TPU v7x, 32 devices: a whole 2x2x4 slice. The times are simulated.
32 devices in a mesh: dp: 16 (over z, y, core), mp: 2 (over x).
Axes of the slice: x: 2, y: 2, z: 4, core: 2. Of those that a mesh axis runs over, the one named last changes fastest.
Arguments:
- state: bfloat16 [32768, 512], P('dp'), may hold values from -6 to 6
- lengths: int32 [32], P('dp'), may hold values from 256 to 1024, as said below
- halt_mask: int32 [32768], P('dp'), may hold values 0 or 1
- w_query: bfloat16 [512, 512], P(None, 'mp'), may hold values from -0.25 to 0.25
- w_key: bfloat16 [512, 512], P(None, 'mp'), may hold values from -0.25 to 0.25
- w_value: bfloat16 [512, 512], P(None, 'mp'), may hold values from -0.25 to 0.25
- w_output: bfloat16 [512, 512], P('mp'), may hold values from -1 to 1
- first_norm_gain: float32 [512], replicated, may hold values from 0.1 to 1.9
- first_norm_bias: float32 [512], replicated, may hold values from -3 to 3
- w_inner: bfloat16 [512, 2048], P(None, 'mp'), may hold values from -0.25 to 0.25
- w_outer: bfloat16 [2048, 512], P('mp'), may hold values from -0.125 to 0.125
- second_norm_gain: float32 [512], replicated, may hold values from 0.1 to 1.9
- second_norm_bias: float32 [512], replicated, may hold values from -3 to 3
- halt_weight: float32 [512], replicated, may hold values from -0.25 to 0.25
- cotangent: bfloat16 [32768, 512], P('dp'), may hold values from -6 to 6
Outputs:
- new_state: float32 [32768, 512], P('dp')
- grad_state: float32 [32768, 512], P('dp')
- grad_query: float32 [512, 512], P(None, 'mp')
- grad_key: float32 [512, 512], P(None, 'mp')
- grad_value: float32 [512, 512], P(None, 'mp')
- grad_output: float32 [512, 512], P('mp')
- first_gain_gradient: float32 [512], replicated
- grad_bias1: float32 [512], replicated
- grad_inner: float32 [512, 2048], P(None, 'mp')
- grad_outer: float32 [2048, 512], P('mp')
- second_gain_gradient: float32 [512], replicated
- grad_bias2: float32 [512], replicated
- grad_halt: float32 [512], replicated
Inputs may be any that keep to these rules, and one draw needn't show every extreme that they name: Tokens of sequence s at positions lengths[s] and beyond are padding; some sequence has exactly 1024 real tokens.
All inputs are finite; a program needn't handle non-finite values. No bound on the sum of `halt_mask` on one device may be relied on, other than what follows from the above.
Results may differ from a plain program's by a relative error of at most 0.017.
The roundings to bfloat16 on the way count: a program that leaves them out, or rounds other values in their place, can miss the bound.
Values sent between devices are 32-bit elements; how exact they have to be, the bound alone decides.
No kernel may reach another device: no remote copies, remote signals or barrier semaphores. Data moves between devices by JAX's collectives and lax.ppermute only.
A program may use at most 256 MiB of HBM per device.

v0:
```python
import math

import jax
import jax.numpy as jnp
from jax import lax
from jax.sharding import PartitionSpec as P

HEAD = 64
LEN = 1024
STEP = 2


def signal_rows(positions, width):
    half = width // 2
    rates = jnp.exp(-math.log(10000.0) * jnp.arange(half, dtype=jnp.float32) / (half - 1))
    angles = positions[:, None] * rates[None, :]
    return jnp.concatenate([jnp.sin(angles), jnp.cos(angles)], axis=1)


def layer_norm_apply(values):
    centre = values - jnp.mean(values, axis=-1, keepdims=True)
    inverse_deviation = lax.rsqrt(jnp.mean(centre * centre, axis=-1) + 1e-05)
    return (centre * inverse_deviation[:, None], inverse_deviation)


def layer_norm_backward(incoming_gradient, centered_normed, inverse_deviation):
    return inverse_deviation[:, None] * (
        incoming_gradient
        - jnp.mean(incoming_gradient, axis=-1, keepdims=True)
        - centered_normed * jnp.mean(incoming_gradient * centered_normed, axis=-1, keepdims=True)
    )


def masked_scores(query4, key4, valid, factor):
    scores = (
        jnp.einsum("sqhd,skhd->shqk", query4, key4, preferred_element_type=jnp.float32) * factor
    )
    return jnp.where(valid[:, None, None, :], scores, jnp.float32(-1e30))


def shards(
    state,
    lengths,
    halt_mask,
    w_query,
    w_key,
    w_value,
    w_output,
    first_norm_gain,
    first_norm_bias,
    w_inner,
    w_outer,
    second_norm_gain,
    second_norm_bias,
    halt_weight,
    cotangent,
):
    rows, width = state.shape
    seqs = rows // LEN
    local = w_query.shape[1]
    heads = local // HEAD
    factor = 1.0 / math.sqrt(HEAD)
    state_full = state.astype(jnp.float32)
    timing = signal_rows(jnp.arange(LEN, dtype=jnp.float32), width) + signal_rows(
        jnp.full((1,), STEP, jnp.float32), width
    )
    embedded_input = (state_full.reshape(seqs, LEN, width) + timing[None]).reshape(rows, width)
    flat_low = embedded_input.astype(jnp.bfloat16)
    query = jnp.dot(flat_low, w_query, preferred_element_type=jnp.float32).astype(jnp.bfloat16)
    key = jnp.dot(flat_low, w_key, preferred_element_type=jnp.float32).astype(jnp.bfloat16)
    value = jnp.dot(flat_low, w_value, preferred_element_type=jnp.float32).astype(jnp.bfloat16)
    query4 = query.reshape(seqs, LEN, heads, HEAD)
    key4 = key.reshape(seqs, LEN, heads, HEAD)
    value4 = value.reshape(seqs, LEN, heads, HEAD)
    valid = jnp.arange(LEN, dtype=jnp.int32)[None, :] < lengths[:, None]
    scores = masked_scores(query4, key4, valid, factor)
    log_total = jax.nn.logsumexp(scores, axis=-1)
    probs_low = jnp.exp(scores - log_total[..., None]).astype(jnp.bfloat16)
    mixed = jnp.einsum("shqk,skhd->sqhd", probs_low, value4, preferred_element_type=jnp.float32)
    mixed_low = mixed.reshape(rows, local).astype(jnp.bfloat16)
    attn_part = jnp.dot(mixed_low, w_output, preferred_element_type=jnp.float32)
    running = halt_mask.astype(jnp.float32)
    attention_output = lax.psum(attn_part, "mp")
    first_centered_normed, first_inverse_deviation = layer_norm_apply(
        embedded_input + attention_output
    )
    first_normed_rows = first_centered_normed * first_norm_gain + first_norm_bias
    normed1_low = first_normed_rows.astype(jnp.bfloat16)
    inner = jnp.dot(normed1_low, w_inner, preferred_element_type=jnp.float32)
    activated = jax.nn.gelu(inner).astype(jnp.bfloat16)
    outer_projection = lax.psum(
        jnp.dot(activated, w_outer, preferred_element_type=jnp.float32), "mp"
    )
    second_centered_normed, second_inverse_deviation = layer_norm_apply(
        first_normed_rows + outer_projection
    )
    block_output = second_centered_normed * second_norm_gain + second_norm_bias
    halt_prob = jax.nn.sigmoid(jnp.sum(block_output * halt_weight, axis=-1))
    new_state = state_full + (running * halt_prob)[:, None] * (block_output - state_full)
    incoming_gradient = cotangent.astype(jnp.float32)
    d_prob = running * jnp.sum(incoming_gradient * (block_output - state_full), axis=-1)
    d_logit = d_prob * halt_prob * (1.0 - halt_prob)
    grad_halt = jnp.sum(d_logit[:, None] * block_output, axis=0)
    grad_block_output = (running * halt_prob)[:, None] * incoming_gradient + d_logit[
        :, None
    ] * halt_weight[None, :]
    second_gain_gradient = jnp.sum(grad_block_output * second_centered_normed, axis=0)
    grad_bias2 = jnp.sum(grad_block_output, axis=0)
    grad_second_hidden = layer_norm_backward(
        grad_block_output * second_norm_gain, second_centered_normed, second_inverse_deviation
    )
    d_outer_low = grad_second_hidden.astype(jnp.bfloat16)
    grad_outer = jnp.dot(activated.T, d_outer_low, preferred_element_type=jnp.float32)
    d_activated = jnp.dot(d_outer_low, w_outer.T, preferred_element_type=jnp.float32)
    gelu_pull = jax.vjp(jax.nn.gelu, inner)[1]
    d_inner_low = gelu_pull(d_activated)[0].astype(jnp.bfloat16)
    grad_inner = jnp.dot(normed1_low.T, d_inner_low, preferred_element_type=jnp.float32)
    grad_first_normed = grad_second_hidden + lax.psum(
        jnp.dot(d_inner_low, w_inner.T, preferred_element_type=jnp.float32), "mp"
    )
    first_gain_gradient = jnp.sum(grad_first_normed * first_centered_normed, axis=0)
    grad_bias1 = jnp.sum(grad_first_normed, axis=0)
    grad_first_hidden = layer_norm_backward(
        grad_first_normed * first_norm_gain, first_centered_normed, first_inverse_deviation
    )
    d_attended_low = grad_first_hidden.astype(jnp.bfloat16)
    grad_output = jnp.dot(mixed_low.T, d_attended_low, preferred_element_type=jnp.float32)
    d_mixed = jnp.dot(d_attended_low, w_output.T, preferred_element_type=jnp.float32).astype(
        jnp.bfloat16
    )
    d_mixed4 = d_mixed.reshape(seqs, LEN, heads, HEAD)
    again = masked_scores(query4, key4, valid, factor)
    probs = jnp.exp(again - log_total[..., None])
    probs_again = probs.astype(jnp.bfloat16)
    d_value = jnp.einsum(
        "shqk,sqhd->skhd", probs_again, d_mixed4, preferred_element_type=jnp.float32
    )
    d_probs = jnp.einsum("sqhd,skhd->shqk", d_mixed4, value4, preferred_element_type=jnp.float32)
    d_scores = (probs * (d_probs - jnp.sum(probs * d_probs, axis=-1, keepdims=True))).astype(
        jnp.bfloat16
    )
    d_query = (
        jnp.einsum("shqk,skhd->sqhd", d_scores, key4, preferred_element_type=jnp.float32) * factor
    )
    d_key = (
        jnp.einsum("shqk,sqhd->skhd", d_scores, query4, preferred_element_type=jnp.float32) * factor
    )
    d_query_low = d_query.reshape(rows, local).astype(jnp.bfloat16)
    d_key_low = d_key.reshape(rows, local).astype(jnp.bfloat16)
    d_value_low = d_value.reshape(rows, local).astype(jnp.bfloat16)
    grad_query = jnp.dot(flat_low.T, d_query_low, preferred_element_type=jnp.float32)
    grad_key = jnp.dot(flat_low.T, d_key_low, preferred_element_type=jnp.float32)
    grad_value = jnp.dot(flat_low.T, d_value_low, preferred_element_type=jnp.float32)
    back_part = jnp.dot(d_query_low, w_query.T, preferred_element_type=jnp.float32)
    back_part = back_part + jnp.dot(d_key_low, w_key.T, preferred_element_type=jnp.float32)
    back_part = back_part + jnp.dot(d_value_low, w_value.T, preferred_element_type=jnp.float32)
    d_embedded = lax.psum(back_part, "mp")
    grad_state = (
        incoming_gradient * (1.0 - running * halt_prob)[:, None] + grad_first_hidden + d_embedded
    )
    (
        grad_query,
        grad_key,
        grad_value,
        grad_output,
        first_gain_gradient,
        grad_bias1,
        grad_inner,
        grad_outer,
        second_gain_gradient,
        grad_bias2,
        grad_halt,
    ) = lax.psum(
        (
            grad_query,
            grad_key,
            grad_value,
            grad_output,
            first_gain_gradient,
            grad_bias1,
            grad_inner,
            grad_outer,
            second_gain_gradient,
            grad_bias2,
            grad_halt,
        ),
        "dp",
    )
    return (
        new_state,
        grad_state,
        grad_query,
        grad_key,
        grad_value,
        grad_output,
        first_gain_gradient,
        grad_bias1,
        grad_inner,
        grad_outer,
        second_gain_gradient,
        grad_bias2,
        grad_halt,
    )


def solution(mesh):
    placed = (
        P("dp", None),
        P("dp"),
        P("dp"),
        P(None, "mp"),
        P(None, "mp"),
        P(None, "mp"),
        P("mp", None),
        P(),
        P(),
        P(None, "mp"),
        P("mp", None),
        P(),
        P(),
        P(),
        P("dp", None),
    )
    return jax.shard_map(
        shards,
        mesh=mesh,
        in_specs=placed,
        out_specs=(
            P("dp", None),
            P("dp", None),
            P(None, "mp"),
            P(None, "mp"),
            P(None, "mp"),
            P("mp", None),
            P(),
            P(),
            P(None, "mp"),
            P("mp", None),
            P(),
            P(),
            P(),
        ),
        check_vma=False,
    )
```

profile of v0, /device:TPU:0, one launch (start us, length us, event | category | flops | bytes accessed | tf_op | source)
XLA Modules:
  0.0 860.7 jit_solution(6632943158825239644)
XLA Ops:
  7.3 0.9 iota_compare_fusion
  8.2 3.8 fusion.31
  12.3 1.3 copy-done.11
  14.4 1.3 copy-done.24
  15.7 1.7 convolution_convert_fusion.1
  17.4 4.6 reshape.196
  21.9 4.1 copy.44
  26.0 3.3 convolution_convert_fusion.2
  29.3 4.5 reshape.195
  33.7 4.1 copy.43
  37.8 3.3 convolution_convert_fusion.3
  41.1 4.4 reshape.194
  45.5 4.1 copy.45
  49.6 15.1 %fusion = (f32[2,4,1024]{2,1,0:T(4,128)S(1)}, f32[2,4,1024,1024]{2,3,1,0:T(8,128)}) fusion(pred[2,1024]{1,0:T(4,128)(4,1)S(1)} %iota_compare_fusion, bf16[2,1024,4,64]{1,3,2,0:T(8,128)(2,1)} %copy.43, bf16[2,1024,4,64]{1,3,2,0:T(8,128)(2,1)} %copy.44), kind=kOutput, calls=%fused_computation.5 | convolution fusion | flops 1098899456 | bytes 35686400 | tf_op jit(solution)/shard_map/sqhd,skhd->shqk/dot_general | solution.py:36
  64.8 14.5 %exponential_reduce_fusion = f32[2,4,1024]{2,1,0:T(4,128)S(1)} fusion(f32[2,4,1024,1024]{2,3,1,0:T(8,128)} %get-tuple-element.47, f32[2,4,1024]{2,1,0:T(4,128)S(1)} %is-finite_select_fusion, pred[2,1024]{1,0:T(4,128)(4,1)S(1)} %iota_compare_fusion), kind=kLoop, calls=%fused_computation.3 | loop fusion | flops 33546240 | bytes 33622016 | tf_op jit(solution)/shard_map/reduce_sum | solution.py:77
  79.4 13.6 %fusion.20 = bf16[2,1024,4,64]{1,3,2,0:T(8,128)(2,1)S(1)} fusion(bf16[2,1024,4,64]{1,3,2,0:T(8,128)(2,1)S(1)} %copy-done.19, f32[2,4,1024,1024]{2,3,1,0:T(8,128)} %get-tuple-element.47, f32[2,4,1024]{2,1,0:T(4,128)S(1)} %log_add_fusion, pred[2,1024]{1,0:T(4,128)(4,1)S(1)} %iota_compare_fusion), kind=kOutput, calls=%fused_computation.59 | convolution fusion | flops 1107820544 | bytes 35686400 | tf_op jit(solution)/shard_map/shqk,skhd->sqhd/dot_general | solution.py:79
  93.0 1.1 copy.47
  94.4 1.0 copy-done.12
  95.4 2.8 fusion.51
  98.2 110.7 %all-reduce.8.cloned.1.call-done = f32[2048,512]{1,0:T(8,128)} async-done(((f32[2048,512]{1,0:T(8,128)}), f32[2048,512]{1,0:T(8,128)}) %all-reduce.8.cloned.1.call-update) | async-done | bytes 4194320 | tf_op jit(solution)/shard_map/psum | solution.py:83
  208.9 3.5 fusion.49
  213.3 1.2 copy-done.46
  214.5 2.6 fusion.42
  217.1 3.2 copy-done.48
  220.3 4.2 fusion.44
  224.6 108.0 %all-reduce.10.cloned.1.call-done = f32[2048,512]{1,0:T(8,128)} async-done(((f32[2048,512]{1,0:T(8,128)}), f32[2048,512]{1,0:T(8,128)}) %all-reduce.10.cloned.1.call-update) | async-done | bytes 4194320 | tf_op jit(solution)/shard_map/psum | solution.py:91
  332.6 4.5 fusion.47
  338.0 2.2 copy-done.9
  340.3 2.0 fusion.12
  342.9 6.1 multiply_reduce_fusion.2
  349.1 9.0 %fusion.8 = bf16[2048,1024]{1,0:T(8,128)(2,1)S(1)} fusion(f32[2048,1024]{1,0:T(8,128)S(1)} %bitcast.88, bf16[1024,512]{1,0:T(8,128)(2,1)S(1)} %copy-done, bf16[2048,512]{1,0:T(8,128)(2,1)S(1)} %copy-done.9, f32[2048]{0:T(1024)S(1)} %broadcast_multiply_fusion.2, f32[2048]{0:T(1024)S(1)} %broadcast_multiply_fusion.3, f32[2048]{0:T(1024)S(1)} %get-tuple-element.43, ...), kind=kOutput, calls=%fused_computation.15 | convolution fusion | flops 2202009600 | bytes 19976192 | tf_op jit(solution)/shard_map/dot_general | solution.py:114
  358.1 2.0 copy-done.49
  360.1 4.5 fusion.52
  364.8 108.0 %all-reduce.12.cloned.1.call-done = f32[2048,512]{1,0:T(8,128)} async-done(((f32[2048,512]{1,0:T(8,128)}), f32[2048,512]{1,0:T(8,128)}) %all-reduce.12.cloned.1.call-update) | async-done | bytes 4194320 | tf_op jit(solution)/shard_map/psum | solution.py:118
  472.7 7.6 multiply_reduce_fusion.3
  480.4 1.8 subtract_multiply_fusion
  482.2 2.0 copy-done.6
  484.9 1.8 reshape.197
  486.7 4.0 copy.49
  490.7 15.6 %fusion.21 = bf16[2,1024,4,64]{1,3,2,0:T(8,128)(2,1)} fusion(bf16[2,1024,4,64]{1,3,2,0:T(8,128)(2,1)} %copy.49, f32[2,4,1024,1024]{2,3,1,0:T(8,128)} %get-tuple-element.47, f32[2,4,1024]{2,1,0:T(4,128)S(1)} %log_add_fusion, pred[2,1024]{1,0:T(4,128)(4,1)S(1)} %iota_compare_fusion), kind=kOutput, calls=%fused_computation.60 | convolution fusion | flops 1107820544 | bytes 35686400 | tf_op jit(solution)/shard_map/shqk,sqhd->skhd/dot_general | solution.py:135
  506.3 24.4 %multiply_reduce_fusion = (f32[2,4,1024]{2,1,0:T(4,128)S(1)}, f32[2,4,1024,1024]{2,3,1,0:T(8,128)}) fusion(f32[2,4,1024,1024]{2,3,1,0:T(8,128)} %get-tuple-element.47, f32[2,4,1024]{2,1,0:T(4,128)S(1)} %log_add_fusion, pred[2,1024]{1,0:T(4,128)(4,1)S(1)} %iota_compare_fusion, bf16[2,1024,4,64]{1,3,2,0:T(8,128)(2,1)} %copy.49, ...), kind=kOutput, calls=%fused_computation.1 | convolution fusion | flops 1115676672 | bytes 69273600 | tf_op jit(solution)/shard_map/sqhd,skhd->shqk/dot_general | solution.py:138
  530.8 27.8 %multiply_convert_fusion = bf16[2,4,1024,1024]{2,3,1,0:T(8,128)(2,1)} fusion(f32[2,4,1024,1024]{2,3,1,0:T(8,128)} %get-tuple-element.49, f32[2,4,1024,1024]{2,3,1,0:T(8,128)} %get-tuple-element.47, f32[2,4,1024]{2,1,0:T(4,128)S(1)} %get-tuple-element.48, f32[2,4,1024]{2,1,0:T(4,128)S(1)} %log_add_fusion, pred[2,1024]{1,0:T(4,128)(4,1)S(1)} %iota_compare_fusion), kind=kLoop, calls=%fused_computation | loop fusion | flops 50331648 | bytes 83953664 | tf_op jit(solution)/shard_map/convert_element_type | solution.py:139
  558.6 12.3 %fusion.23 = bf16[2,1024,4,64]{1,3,2,0:T(8,128)(2,1)} fusion(bf16[2,1024,4,64]{1,3,2,0:T(8,128)(2,1)} %copy.43, bf16[2,4,1024,1024]{2,3,1,0:T(8,128)(2,1)} %multiply_convert_fusion), kind=kOutput, calls=%fused_computation.62 | convolution fusion | flops 1074790400 | bytes 18874368 | tf_op jit(solution)/shard_map/shqk,sqhd->skhd/dot_general | solution.py:146
  570.9 8.9 %fusion.22 = bf16[2,1024,4,64]{1,3,2,0:T(8,128)(2,1)S(1)} fusion(bf16[2,1024,4,64]{1,3,2,0:T(8,128)(2,1)S(1)} %copy-done.14, bf16[2,4,1024,1024]{2,3,1,0:T(8,128)(2,1)} %multiply_convert_fusion), kind=kOutput, calls=%fused_computation.61 | convolution fusion | flops 1074790400 | bytes 18874368 | tf_op jit(solution)/shard_map/shqk,skhd->sqhd/dot_general | solution.py:143
  579.8 1.1 copy.59
  581.2 1.1 copy.53
  582.6 1.1 copy.56
  586.0 3.1 add_add_fusion
  589.2 7.4 fusion.40
  596.6 11.4 %fusion.27 = f32[1024,512]{1,0:T(8,128)} fusion(f32[2048,1024]{1,0:T(8,128)} %copy-done.48, bf16[2048,512]{1,0:T(8,128)(2,1)S(1)} %copy-done.10, f32[2048]{0:T(1024)S(1)} %broadcast_multiply_fusion.2, f32[2048]{0:T(1024)S(1)} %broadcast_multiply_fusion.3, f32[2048]{0:T(1024)S(1)} %get-tuple-element.43, f32[2048]{0:T(1024)S(1)} %get-tuple-element.36, ...), kind=kOutput, calls=%fused_computation.66 | convolution fusion | flops 2178940928 | bytes 16830464 | tf_op jit(solution)/shard_map/dot_general | solution.py:113
  608.0 1.6 fusion.57
  609.6 1.6 fusion.56
  611.2 1.6 fusion.55
  612.8 1.6 fusion.24
  615.1 61.1 %all-reduce = (f32[512]{0:T(512)}, f32[512]{0:T(512)}, f32[512]{0:T(512)}, f32[512]{0:T(512)}, f32[512]{0:T(512)}) all-reduce(f32[512]{0:T(512)S(1)} %get-tuple-element.13, f32[512]{0:T(512)S(1)} %get-tuple-element.21, f32[512]{0:T(512)S(1)} %copy-done.41, f32[512]{0:T(512)S(1)} %copy-done.43, ...), channel_id=1, replica_groups=mesh['dp'=16,'mp'=2] {'dp'}, use_global_device_ids=true, to_apply=%region_22.23 | all-reduce | flops 2560 | bytes 20480 | tf_op jit(solution)/shard_map/psum | solution.py:173
  676.2 21.0 %all-reduce.14.cloned.1.call-done = f32[2048,512]{1,0:T(8,128)} async-done(((f32[2048,512]{1,0:T(8,128)}), f32[2048,512]{1,0:T(8,128)}) %all-reduce.14.cloned.1.call-update) | async-done | bytes 4194320 | tf_op jit(solution)/shard_map/psum | solution.py:157
  697.2 6.1 fusion.10
  703.3 140.3 %all-reduce.16.cloned.1.call-done = (f32[512,256]{1,0:T(8,128)}, f32[512,256]{1,0:T(8,128)}, f32[512,256]{1,0:T(8,128)}, f32[256,512]{1,0:T(8,128)}, f32[512,1024]{1,0:T(8,128)}, /*index=5*/f32[1024,512]{1,0:T(8,128)}) async-done(((f32[512,256]{1,0:T(8,128)}, f32[512,256]{1,0:T(8,128)}, f32[512,256]{1,0:T(8,128)}, f32[256,512]{1,0:T(8,128)}, f32[512,1024]{1,0:T(8,128)}, /*index=5*/f32[1024,512]{1,0:T(8,128)}), ...) | async-done | bytes 6291472 | tf_op jit(solution)/shard_map/psum | solution.py:173
  843.6 2.0 copy.86
  845.6 1.9 copy.87
  847.5 1.9 copy.88
  849.3 2.0 copy.89
  851.3 1.3 copy.90
  852.6 1.3 copy.91
  (132 shorter events, 8.5 us)
Async XLA Ops:
  7.2 213.1 %copy-start = (bf16[1024,512]{1,0:T(8,128)(2,1)S(1)}, bf16[1024,512]{1,0:T(8,128)(2,1)}, u32[]{:S(2)}) copy-start(bf16[1024,512]{1,0:T(8,128)(2,1)} %param.25) | copy-start | bytes 3145732
  7.2 6.5 copy-start.8
  7.2 201.7 %all-reduce.8.cloned.1.call-start = ((), (), s32[]{:S(2)}) async-start(), calls=%async_computation | async-start | bytes 8388608 | tf_op jit(solution)/shard_map/psum | solution.py:83
  12.3 1.3 copy-start.11
  13.6 2.0 copy-start.32
  14.4 1.3 copy-start.24
  17.4 8.6 %copy-start.30 = (bf16[512,256]{1,0:T(8,128)(2,1)S(1)}, bf16[512,256]{1,0:T(8,128)(2,1)}, u32[]{:S(2)}) copy-start(bf16[512,256]{1,0:T(8,128)(2,1)} %param.18) | copy-start | bytes 786436
  29.3 8.6 copy-start.34
  64.8 14.6 %copy-start.19 = (bf16[2,1024,4,64]{1,3,2,0:T(8,128)(2,1)S(1)}, bf16[2,1024,4,64]{1,3,2,0:T(8,128)(2,1)}, u32[]{:S(2)}) copy-start(bf16[2,1024,4,64]{1,3,2,0:T(8,128)(2,1)} %copy.45) | copy-start | bytes 3145732
  93.0 2.4 copy-start.29
  94.4 1.0 copy-start.12
  98.1 234.5 %all-reduce.10.cloned.1.call-start = ((), (), s32[]{:S(2)}) async-start(), calls=%async_computation.1 | async-start | bytes 8388608 | tf_op jit(solution)/shard_map/psum | solution.py:91
  212.4 4.7 copy-start.4
  212.4 0.9 copy-start.39
  212.4 0.9 copy-start.45
  212.4 2.1 copy-start.46
  217.1 3.2 copy-start.48
  224.6 248.1 %all-reduce.12.cloned.1.call-start = ((), (), s32[]{:S(2)}) async-start(), calls=%async_computation.2 | async-start | bytes 8388608 | tf_op jit(solution)/shard_map/psum | solution.py:118
  337.1 11.9 %copy-start.2 = (f32[2048,512]{1,0:T(8,128)}, f32[2048,512]{1,0:T(8,128)S(1)}, u32[]{:S(2)}) copy-start(f32[2048,512]{1,0:T(8,128)S(1)} %get-tuple-element.39) | copy-start | bytes 12582916
  337.1 3.1 copy-start.9
  337.1 3.1 copy-start.37
  337.2 3.1 copy-start.38
  337.2 3.1 copy-start.40
  340.2 2.1 copy-start.44
  340.3 8.8 %slice-start = ((s8[8388608]{0:T(1024)(128)(4,1)}), s8[4194304]{0:T(1024)(128)(4,1)S(1)}, s32[]{:S(2)}) async-start(s8[8388608]{0:T(1024)(128)(4,1)} %bitcast.87), calls=%async_computation.5 | async-start | bytes 8388608
  342.9 6.1 slice-start.1
  349.0 11.1 %copy-start.47 = (bf16[512,1024]{1,0:T(8,128)(2,1)S(1)}, bf16[512,1024]{1,0:T(8,128)(2,1)}, u32[]{:S(2)}) copy-start(bf16[512,1024]{1,0:T(8,128)(2,1)} %param.24) | copy-start | bytes 3145732
  358.1 2.0 copy-start.49
  364.7 108.0 %copy-start.10 = (bf16[2048,512]{1,0:T(8,128)(2,1)S(1)}, bf16[2048,512]{1,0:T(8,128)(2,1)}, u32[]{:S(2)}) copy-start(bf16[2048,512]{1,0:T(8,128)(2,1)} %param.29) | copy-start | bytes 6291460
  364.7 332.5 %all-reduce.14.cloned.1.call-start = ((), (), s32[]{:S(2)}) async-start(), calls=%async_computation.3 | async-start | bytes 8388608 | tf_op jit(solution)/shard_map/psum | solution.py:157
  472.7 7.6 copy-start.5
  482.1 2.0 copy-start.6
  490.7 15.6 %copy-start.20 = (bf16[2,1024,4,64]{1,3,2,0:T(8,128)(2,1)S(1)}, bf16[2,1024,4,64]{1,3,2,0:T(8,128)(2,1)}, u32[]{:S(2)}) copy-start(bf16[2,1024,4,64]{1,3,2,0:T(8,128)(2,1)} %copy.45) | copy-start | bytes 3145732
  558.5 12.3 %copy-start.14 = (bf16[2,1024,4,64]{1,3,2,0:T(8,128)(2,1)S(1)}, bf16[2,1024,4,64]{1,3,2,0:T(8,128)(2,1)}, u32[]{:S(2)}) copy-start(bf16[2,1024,4,64]{1,3,2,0:T(8,128)(2,1)} %copy.44) | copy-start | bytes 3145732
  570.9 8.9 %copy-start.28 = (bf16[2,1024,4,64]{1,3,2,0:T(8,128)(2,1)S(1)}, bf16[2,1024,4,64]{1,3,2,0:T(8,128)(2,1)}, u32[]{:S(2)}) copy-start(bf16[2,1024,4,64]{1,3,2,0:T(8,128)(2,1)} %fusion.21) | copy-start | bytes 3145732
  579.8 2.8 copy-start.21
  581.2 4.7 copy-start.22
  581.2 2.8 copy-start.31
  582.6 2.2 copy-start.15
  583.9 1.1 copy-start.17
  584.0 1.1 copy-start.33
  585.1 0.9 copy-start.35
  589.1 254.4 %all-reduce.16.cloned.1.call-start = ((), (), s32[]{:S(2)}) async-start(), calls=%async_computation.4 | async-start | bytes 12582912 | tf_op jit(solution)/shard_map/psum | solution.py:173
  589.2 7.4 copy-start.3
  596.6 11.4 %copy-start.23 = (bf16[32,8,2,1024]{3,1,2,0:T(8,128)(2,1)S(1)}, bf16[32,8,2,1024]{3,1,2,0:T(8,128)(2,1)}, u32[]{:S(2)}) copy-start(bf16[32,8,2,1024]{3,1,2,0:T(8,128)(2,1)} %copy-done.22) | copy-start | bytes 3145732
  596.6 11.4 %copy-start.25 = (bf16[2048,512]{1,0:T(8,128)(2,1)S(1)}, bf16[2048,512]{1,0:T(8,128)(2,1)}, u32[]{:S(2)}) copy-start(bf16[2048,512]{1,0:T(8,128)(2,1)} %copy-done.24) | copy-start | bytes 6291460
  596.6 13.0 %copy-start.18 = (bf16[32,8,2,1024]{3,1,2,0:T(8,128)(2,1)S(1)}, bf16[32,8,2,1024]{3,1,2,0:T(8,128)(2,1)}, u32[]{:S(2)}) copy-start(bf16[32,8,2,1024]{3,1,2,0:T(8,128)(2,1)} %copy-done.17) | copy-start | bytes 3145732
  608.0 3.2 copy-start.16
  609.6 3.2 copy-start.7
  609.6 3.2 copy-start.13
  614.3 0.7 copy-start.41
  614.3 0.7 copy-start.42
  614.3 0.7 copy-start.43
  614.3 82.8 %copy-start.36 = (f32[2048]{0:T(1024)S(1)}, f32[2048]{0:T(1024)}, u32[]{:S(2)}) copy-start(f32[2048]{0:T(1024)} %get-tuple-element.35) | copy-start | bytes 24580
  843.6 7.7 copy-start.27
  843.6 9.0 %copy-start.26 = (f32[1024,512]{1,0:T(8,128)S(1)}, f32[1024,512]{1,0:T(8,128)}, u32[]{:S(2)}) copy-start(f32[1024,512]{1,0:T(8,128)} %get-tuple-element.61) | copy-start | bytes 6291460
  849.3 4.6 copy-start.1
Sparse Core Ops, SparseCore 0:
  98.3 110.5 all-reduce.7
  224.7 107.8 all-reduce.9
  364.8 107.8 all-reduce.11
  589.3 107.8 all-reduce.13
  702.5 141.0 all-reduce.15
where the time goes:
time: 867 us; the launch traced here: 861 us
  waiting for transfers between devices  488 us (56%)
  matrix products  152 us (18%)
  other arithmetic  82 us (9%)
  local copies, waits for them, and re-layouts  62.9 us (7%)
  blocking collectives  61.1 us (7%)
  between operations  14.7 us (2%)
    psum x1, waiting for transfers between devices, shards(): lax.psum((grad_query, grad_key, grad_value, grad_output, first_gain_gradi...  140 us
    psum x1, waiting for transfers between devices, shards(): attention_output = lax.psum(attn_part, 'mp')  111 us
    psum x1, waiting for transfers between devices, shards(): lax.psum(jnp.dot(activated, w_outer, preferred_element_type=jnp.float32),...  108 us
    psum x1, waiting for transfers between devices, shards(): lax.psum(jnp.dot(d_inner_low, w_inner.T, preferred_element_type=jnp.float...  108 us
    psum x1, blocking collectives, shards(): lax.psum((grad_query, grad_key, grad_value, grad_output, first_gain_gradi...  61.1 us
    convert_element_type x1, other arithmetic, shards(): (probs * (d_probs - jnp.sum(probs * d_probs, axis=-1, keepdims=True))).as...  27.8 us
    unnamed x114, local copies, waits for them, and re-layouts  27 us
    dot_general x1, matrix products, shards(): jnp.einsum('sqhd,skhd->shqk', d_mixed4, value4, preferred_element_type=jn...  24.4 us
  transfers between devices with their start and end apart: 5, of which 5 were waited for; matrix products, arithmetic and copies ran while one was open for 4% of the time, Pallas kernels for 0%

commit v1 on v0

v1 whole, which is shorter than its diff:
```python
import functools
import math

import jax
import jax.numpy as jnp
import numpy as np
from jax import lax
from jax.experimental import pallas as pl
from jax.experimental.pallas import tpu as pltpu
from jax.sharding import PartitionSpec as P

HEAD = 64
LEN = 1024
STEP = 2
LOG2E = 1.4426950408889634
BF = jnp.bfloat16
F32 = jnp.float32
NN = (((1,), (0,)), ((), ()))
NT = (((1,), (1,)), ((), ()))
TN = (((0,), (0,)), ((), ()))
TT = (((0,), (1,)), ((), ()))
VMEM_LIMIT = 60 << 20
CHUNK = 256


def mm(a, b, dims=NN):
    return lax.dot_general(a, b, dims, preferred_element_type=F32)


def params():
    return pltpu.CompilerParams(vmem_limit_bytes=VMEM_LIMIT)


def whole(shape):
    zeros = (0,) * len(shape)
    return pl.BlockSpec(shape, lambda *_: zeros)


def timing_rows(width):
    half = width // 2
    rates = np.exp(-math.log(10000.0) * np.arange(half, dtype=np.float64) / (half - 1))

    def rows(positions):
        angles = positions[:, None] * rates[None, :]
        return np.concatenate([np.sin(angles), np.cos(angles)], axis=1)

    return (rows(np.arange(LEN, dtype=np.float64)) + rows(np.array([float(STEP)]))).astype(
        np.float32
    )


def split_low(value):
    high = value.astype(BF)
    return high, (value - high.astype(F32)).astype(BF)


def rolled(pair):
    return jnp.concatenate([pair[:, HEAD:], pair[:, :HEAD]], axis=1)


def lane_index(shape):
    return lax.broadcasted_iota(jnp.int32, shape, 1)


def row_index(shape):
    return lax.broadcasted_iota(jnp.int32, shape, 0)


def attention_forward_kernel(
    lengths, state, timing, wq, wk, wv, e_out, mixed_out, r_out,
    kaug, qaug, vaug, sa, sb, ma, mb, *, seqs, heads
):
    count = seqs * heads
    j = pl.program_id(0)
    pieces = LEN // CHUNK

    def score_piece(i, c, target):
        rows = slice(c * CHUNK, (c + 1) * CHUNK)
        s = mm(kaug[i, rows], qaug[i])
        target[rows] = s
        return jnp.max(s.reshape(CHUNK // 8, 8, LEN), axis=0)

    @pl.when(j == 0)
    def _():
        for s in range(seqs):
            x = (state[s * LEN : (s + 1) * LEN].astype(F32) + timing[...]).astype(BF)
            query = mm(wq[...], x, TT).astype(BF).astype(F32) * (LOG2E / math.sqrt(HEAD))
            high, rest = split_low(query)
            key = mm(x, wk[...]).astype(BF)
            value = mm(wv[...], x, TT).astype(BF)
            shape = (LEN, 2 * HEAD)
            lane = lane_index(shape)
            padded = row_index(shape) >= lengths[s]
            mask = jnp.where(padded & ((lane == 0) | (lane == HEAD)), -1e30, 0.0).astype(BF)
            first = row_index((HEAD, LEN)) == 0
            ones = jnp.where(first, 1.0, 0.0).astype(BF)
            zeros = jnp.zeros((HEAD, LEN), BF)
            for h in range(heads):
                i = s * heads + h
                pair = key[:, (h // 2) * 128 : (h // 2) * 128 + 128]
                turned = rolled(pair)
                mine = slice(h * HEAD, (h + 1) * HEAD)
                kaug[i, :, 0:128] = pair
                if h % 2 == 0:
                    kaug[i, :, 128:256] = jnp.where(lane < HEAD, mask, turned)
                    parts = (high[mine], zeros, ones, rest[mine])
                else:
                    kaug[i, :, 128:256] = jnp.where(lane < HEAD, turned, mask)
                    parts = (zeros, high[mine], rest[mine], ones)
                for n, part in enumerate(parts):
                    qaug[i, n * HEAD : (n + 1) * HEAD] = part
                vaug[i, 0:HEAD] = value[mine]
                vaug[i, HEAD : HEAD + 16] = jnp.ones((16, LEN), BF)
        top = None
        for c in range(pieces):
            m = score_piece(0, c, sa)
            top = m if top is None else jnp.maximum(top, m)
        ma[...] = jnp.max(top, axis=0, keepdims=True)

    def step(slot, cur, cur_m, nxt, nxt_m):
        i = 2 * j + slot
        following = lax.rem(i + 1, count)
        shift = cur_m[...]
        top = None
        out = None
        for c in range(pieces):
            rows = slice(c * CHUNK, (c + 1) * CHUNK)
            m = score_piece(following, c, nxt)
            top = m if top is None else jnp.maximum(top, m)
            e = jnp.exp2(cur[rows] - shift).astype(BF)
            e_out[slot, rows] = e
            o = mm(vaug[i, :, rows], e)
            out = o if out is None else out + o
        nxt_m[...] = jnp.max(top, axis=0, keepdims=True)
        r = 1.0 / out[HEAD : HEAD + 1]
        mixed_out[slot * HEAD : (slot + 1) * HEAD] = (out[:HEAD] * r).astype(BF)
        r_out[slot] = r

    step(0, sa, ma, sb, mb)
    step(1, sb, mb, sa, ma)


def attention_forward(lengths, state, timing, wq, wk, wv):
    rows, width = state.shape
    seqs, local = rows // LEN, wq.shape[1]
    heads = local // HEAD
    count, half = seqs * heads, heads // 2
    return pl.pallas_call(
        functools.partial(attention_forward_kernel, seqs=seqs, heads=heads),
        grid=(count // 2,),
        in_specs=[
            pl.BlockSpec(memory_space=pltpu.SMEM),
            whole((rows, width)),
            whole((LEN, width)),
            whole((width, local)),
            whole((width, local)),
            whole((width, local)),
        ],
        out_specs=[
            pl.BlockSpec((2, LEN, LEN), lambda j: (j, 0, 0)),
            pl.BlockSpec((2 * HEAD, LEN), lambda j: (j % half, j // half)),
            pl.BlockSpec((2, 1, LEN), lambda j: (j, 0, 0)),
        ],
        out_shape=[
            jax.ShapeDtypeStruct((count, LEN, LEN), BF),
            jax.ShapeDtypeStruct((local, rows), BF),
            jax.ShapeDtypeStruct((count, 1, LEN), F32),
        ],
        scratch_shapes=[
            pltpu.VMEM((count, LEN, 256), BF),
            pltpu.VMEM((count, 256, LEN), BF),
            pltpu.VMEM((count, HEAD + 16, LEN), BF),
            pltpu.VMEM((LEN, LEN), F32),
            pltpu.VMEM((LEN, LEN), F32),
            pltpu.VMEM((1, LEN), F32),
            pltpu.VMEM((1, LEN), F32),
        ],
        compiler_params=params(),
        cost_estimate=pl.CostEstimate(
            flops=8 * 2 * count * LEN * LEN * HEAD,
            bytes_accessed=2 * count * LEN * LEN,
            transcendentals=count * LEN * LEN,
        ),
        name="attention_forward",
    )(lengths, state, timing, wq, wk, wv)


def row_mean(v):
    return jnp.mean(v, axis=-1, keepdims=True)


def norm_rows(v):
    centre = v - row_mean(v)
    deviation = lax.rsqrt(row_mean(centre * centre) + 1e-05)
    return centre * deviation, deviation


def norm_back(e, xhat, deviation):
    return deviation * (e - row_mean(e) - xhat * row_mean(e * xhat))


def fold_rows(v):
    return jnp.sum(v.reshape(v.shape[0] // 8, 8, v.shape[1]), axis=0)


def middle_kernel(
    state, timing, cot, run, mix_a, mix_b, r_a, r_b, wo_a, wo_b, wi_a, wi_b, wu_a, wu_b,
    vectors, new_state, gs, do_a, do_b, dl_a, dl_b, grads, act, slope, fold, *, heads
):
    t = pl.program_id(0)
    last = pl.num_programs(0) - 1
    ff = wi_a.shape[1]
    local = wo_a.shape[0]
    width = state.shape[1]
    gain1, bias1, gain2, bias2, halt_w = (vectors[n : n + 1] for n in range(5))

    @pl.when(t == 0)
    def _():
        grads[...] = jnp.zeros(grads.shape, F32)
        fold[...] = jnp.zeros(fold.shape, F32)

    old = state[...].astype(F32)
    embedded = old + timing[...]
    attended = mm(mix_a[...], wo_a[...], TN) + mm(mix_b[...], wo_b[...], TN)
    xhat1, dev1 = norm_rows(embedded + attended)
    normed1 = xhat1 * gain1 + bias1
    low1 = normed1.astype(BF)
    c0 = math.sqrt(2.0 / math.pi)
    outer = None
    for n, (wi, wu) in enumerate(((wi_a, wu_a), (wi_b, wu_b))):
        v = mm(low1, wi[...])
        square = v * v
        h = 0.5 + 0.5 * jnp.tanh(v * (c0 + (c0 * 0.044715) * square))
        g = v * h
        act[n] = g.astype(BF)
        slope[n] = (
            h + g * (1.0 - h) * (2.0 * c0 + (6.0 * c0 * 0.044715) * square)
        ).astype(slope.dtype)
        o = mm(act[n], wu[...])
        outer = o if outer is None else outer + o
    xhat2, dev2 = norm_rows(normed1 + outer)
    block = xhat2 * gain2 + bias2
    halt = jax.nn.sigmoid(jnp.sum(block * halt_w, axis=-1, keepdims=True))
    running = run[...].astype(F32)
    gate = running * halt
    new_state[...] = old + gate * (block - old)
    g_in = cot[...].astype(F32)
    d_prob = running * jnp.sum(g_in * (block - old), axis=-1, keepdims=True)
    d_logit = d_prob * halt * (1.0 - halt)
    d_block = gate * g_in + d_logit * halt_w
    fold[4] += fold_rows(d_logit * block)
    fold[2] += fold_rows(d_block * xhat2)
    fold[3] += fold_rows(d_block)
    d_hidden2 = norm_back(d_block * gain2, xhat2, dev2)
    d_outer = d_hidden2.astype(BF)
    d_normed1 = d_hidden2
    for n, (wi, wu) in enumerate(((wi_a, wu_a), (wi_b, wu_b))):
        d_act = mm(d_outer, wu[...], NT)
        d_inner = (d_act * slope[n].astype(F32)).astype(BF)
        d_normed1 = d_normed1 + mm(d_inner, wi[...], NT)
        if n == 0:
            grads[0:ff] += mm(act[0], d_outer, TN)
            gi = mm(low1, d_inner, TN)
            for p in range(ff // width):
                grads[ff + p * width : ff + (p + 1) * width] += gi[
                    :, p * width : (p + 1) * width
                ]
    fold[0] += fold_rows(d_normed1 * xhat1)
    fold[1] += fold_rows(d_normed1)
    d_hidden1 = norm_back(d_normed1 * gain1, xhat1, dev1)
    d_att = d_hidden1.astype(BF)
    gs[...] = g_in * (1.0 - gate) + d_hidden1
    grads[2 * ff : 2 * ff + local] += mm(mix_a[...], d_att)
    for mix, r, wo, do, dl in (
        (mix_a, r_a, wo_a, do_a, dl_a),
        (mix_b, r_b, wo_b, do_b, dl_b),
    ):
        d_mixed = mm(wo[...], d_att, NT).astype(BF).astype(F32)
        for h in range(heads):
            mine = slice(h * HEAD, (h + 1) * HEAD)
            part = d_mixed[mine]
            scale = r[h]
            do[mine] = part * scale
            total = jnp.sum(part * mix[mine].astype(F32), axis=0, keepdims=True)
            dl[h] = total * scale

    @pl.when(t == last)
    def _():
        base = 2 * ff + local
        for n in range(5):
            grads[base + n : base + n + 1] = jnp.sum(fold[n], axis=0, keepdims=True)


def middle(state, timing, cot, run, mix_a, mix_b, r_a, r_b, wo_a, wo_b, wi_a, wi_b, wu_a,
           wu_b, vectors):
    rows, width = state.shape
    local, ff = wo_a.shape[0], wi_a.shape[1]
    heads = local // HEAD
    tile = 512
    per = LEN // tile
    grad_rows = 2 * ff + local + 8
    by_rows = pl.BlockSpec((tile, width), lambda t: (t, 0))
    by_columns = pl.BlockSpec((local, tile), lambda t: (0, t))
    per_head = pl.BlockSpec((heads, 1, tile), lambda t: (t // per, 0, t % per))
    return pl.pallas_call(
        functools.partial(middle_kernel, heads=heads),
        grid=(rows // tile,),
        in_specs=[
            by_rows,
            pl.BlockSpec((tile, width), lambda t: (t % per, 0)),
            by_rows,
            pl.BlockSpec((tile, 1), lambda t: (t, 0)),
            by_columns,
            by_columns,
            per_head,
            per_head,
            whole((local, width)),
            whole((local, width)),
            whole((width, ff)),
            whole((width, ff)),
            whole((ff, width)),
            whole((ff, width)),
            whole((8, width)),
        ],
        out_specs=[
            by_rows,
            by_rows,
            by_columns,
            by_columns,
            per_head,
            per_head,
            whole((grad_rows, width)),
        ],
        out_shape=[
            jax.ShapeDtypeStruct((rows, width), F32),
            jax.ShapeDtypeStruct((rows, width), F32),
            jax.ShapeDtypeStruct((local, rows), F32),
            jax.ShapeDtypeStruct((local, rows), F32),
            jax.ShapeDtypeStruct((rows // LEN * heads, 1, LEN), F32),
            jax.ShapeDtypeStruct((rows // LEN * heads, 1, LEN), F32),
            jax.ShapeDtypeStruct((grad_rows, width), F32),
        ],
        scratch_shapes=[
            pltpu.VMEM((2, tile, ff), BF),
            pltpu.VMEM((2, tile, ff), F32),
            pltpu.VMEM((8, 8, width), F32),
        ],
        compiler_params=params(),
        cost_estimate=pl.CostEstimate(
            flops=2 * rows * width * ff * 10 + 2 * rows * width * local * 6,
            bytes_accessed=rows * width * 20,
            transcendentals=2 * rows * ff,
        ),
        name="middle",
    )(state, timing, cot, run, mix_a, mix_b, r_a, r_b, wo_a, wo_b, wi_a, wi_b, wu_a, wu_b,
      vectors)


def attention_backward_kernel(
    e_in, do_in, dl_in, state, timing, wq, wk, wv, gs_in, gs_out, *rest, heads, own
):
    if own:
        gq, gk, gv, x_s, qt, kt, vaug, dq, dk, dv, aq, akv = rest
    else:
        x_s, qt, kt, vaug, dq, dk, dv = rest
    i = pl.program_id(0)
    h = lax.rem(i, heads)
    factor = 1.0 / math.sqrt(HEAD)
    pieces = LEN // CHUNK
    local = wq.shape[1]

    @pl.when(h == 0)
    def _():
        x = (state[...].astype(F32) + timing[...]).astype(BF)
        x_s[...] = x
        query = mm(wq[...], x, TT).astype(BF)
        key = mm(wk[...], x, TT).astype(BF)
        value = mm(x, wv[...]).astype(BF)
        lane = lane_index((LEN, 2 * HEAD))
        ones = jnp.where((lane % HEAD) < 3, 1.0, 0.0).astype(BF)
        for n in range(heads):
            mine = slice(n * HEAD, (n + 1) * HEAD)
            qt[n] = query[mine]
            kt[n] = key[mine]
            pair = value[:, (n // 2) * 128 : (n // 2) * 128 + 128]
            turned = rolled(pair)
            if n % 2 == 0:
                vaug[n, :, 0:128] = jnp.where(lane < HEAD, pair, turned)
            else:
                vaug[n, :, 0:128] = jnp.where(lane < HEAD, turned, pair)
            vaug[n, :, 128:256] = ones

    high, low = split_low(do_in[...])
    delta = -dl_in[0]
    d1 = delta.astype(BF)
    left = delta - d1.astype(F32)
    d2 = left.astype(BF)
    d3 = (left - d2.astype(F32)).astype(BF)
    index = row_index((2 * HEAD, LEN))
    tail = jnp.where(
        index == 0,
        d1.astype(F32),
        jnp.where(index == 1, d2.astype(F32), jnp.where(index == 2, d3.astype(F32), 0.0)),
    ).astype(BF)
    right = jnp.concatenate([high, low, tail], axis=0)
    query = qt[h]
    out = None
    for c in range(pieces):
        rows = slice(c * CHUNK, (c + 1) * CHUNK)
        d_probs = mm(vaug[h, rows], right)
        e = e_in[0, rows]
        d_scores = (e.astype(F32) * d_probs).astype(BF)
        dv[h, rows] = mm(e, high, NT).astype(BF)
        dk[h, rows] = (mm(d_scores, query, NT) * factor).astype(BF)
        o = mm(kt[h, :, rows], d_scores)
        out = o if out is None else out + o
    dq[pl.ds(pl.multiple_of(h * HEAD, HEAD), HEAD)] = (out * factor).astype(BF)

    @pl.when(h == heads - 1)
    def _():
        x = x_s[...]
        d_query = dq[...]
        d_key = jnp.concatenate([dk[n] for n in range(heads)], axis=1)
        d_value = jnp.concatenate([dv[n] for n in range(heads)], axis=1)
        total = mm(d_query, wq[...], TT)
        total = total + mm(d_key, wk[...], NT)
        total = total + mm(d_value, wv[...], NT)
        gs_out[...] = gs_in[...] + total
        if own:
            g1 = mm(d_query, x)
            g2 = mm(x, jnp.concatenate([d_key, d_value], axis=1), TN)

            @pl.when(i < heads)
            def _():
                aq[...] = g1
                akv[...] = g2

            @pl.when(i >= heads)
            def _():
                aq[...] += g1
                akv[...] += g2

            @pl.when(i == pl.num_programs(0) - 1)
            def _():
                gq[...] = aq[...].T
                gk[...] = akv[:, :local]
                gv[...] = akv[:, local:]


def attention_backward(e, do, dl, state, timing, wq, wk, wv, gs, own):
    rows, width = state.shape
    seqs, local = rows // LEN, wq.shape[1]
    heads = local // HEAD
    count = seqs * heads
    by_rows = pl.BlockSpec((LEN, width), lambda i: (i // heads, 0))
    out_specs = [by_rows]
    out_shape = [jax.ShapeDtypeStruct((rows, width), F32)]
    scratch = [
        pltpu.VMEM((LEN, width), BF),
        pltpu.VMEM((heads, HEAD, LEN), BF),
        pltpu.VMEM((heads, HEAD, LEN), BF),
        pltpu.VMEM((heads, LEN, 256), BF),
        pltpu.VMEM((local, LEN), BF),
        pltpu.VMEM((heads, LEN, HEAD), BF),
        pltpu.VMEM((heads, LEN, HEAD), BF),
    ]
    if own:
        out_specs += [whole((width, local))] * 3
        out_shape += [jax.ShapeDtypeStruct((width, local), F32)] * 3
        scratch += [pltpu.VMEM((local, width), F32), pltpu.VMEM((width, 2 * local), F32)]
    return pl.pallas_call(
        functools.partial(attention_backward_kernel, heads=heads, own=own),
        grid=(count,),
        in_specs=[
            pl.BlockSpec((1, LEN, LEN), lambda i: (i, 0, 0)),
            pl.BlockSpec((HEAD, LEN), lambda i: (i % heads, i // heads)),
            pl.BlockSpec((1, 1, LEN), lambda i: (i, 0, 0)),
            by_rows,
            whole((LEN, width)),
            whole((width, local)),
            whole((width, local)),
            whole((width, local)),
            by_rows,
        ],
        out_specs=out_specs,
        out_shape=out_shape,
        scratch_shapes=scratch,
        compiler_params=params(),
        input_output_aliases={8: 0},
        cost_estimate=pl.CostEstimate(
            flops=16 * 2 * count * LEN * LEN * HEAD,
            bytes_accessed=2 * count * LEN * LEN,
            transcendentals=0,
        ),
        name="attention_backward_own" if own else "attention_backward_other",
    )(e, do, dl, state, timing, wq, wk, wv, gs)


def pack_kernel(place, wq, wk, wv, wo, wi, wu, out_a, out_b):
    p = place[0]
    width, local = wq.shape
    quarter = width // 4

    def cut(ref, size):
        return ref[pl.ds(pl.multiple_of(p * size, size), size)].astype(F32)

    for n, ref in enumerate((wq, wk, wv)):
        out_a[:, n * local : (n + 1) * local] = cut(ref, quarter)
    inner = cut(wi, quarter)
    for n in range(wi.shape[1] // width):
        out_b[n * quarter : (n + 1) * quarter] = inner[:, n * width : (n + 1) * width]
    base = quarter * (wi.shape[1] // width)
    fourth = wu.shape[0] // 4
    out_b[base : base + fourth] = cut(wu, fourth)
    out_b[base + fourth :] = cut(wo, wo.shape[0] // 4)


def pack(place, wq, wk, wv, wo, wi, wu):
    width, local = wq.shape
    ff = wi.shape[1]
    return pl.pallas_call(
        pack_kernel,
        in_specs=[pl.BlockSpec(memory_space=pltpu.SMEM)]
        + [pl.BlockSpec(memory_space=pltpu.VMEM)] * 6,
        out_specs=[pl.BlockSpec(memory_space=pltpu.VMEM)] * 2,
        out_shape=[
            jax.ShapeDtypeStruct((width // 4, 3 * local), F32),
            jax.ShapeDtypeStruct((ff // 2 + local // 4, width), F32),
        ],
        compiler_params=params(),
        name="pack",
    )(place, wq, wk, wv, wo, wi, wu)


def unpack_qkv_kernel(place, a, b, c, d, wq, wk, wv):
    quarter = a.shape[0]
    local = wq.shape[1]
    for flip, ref in ((0, a), (2, b), (1, c), (3, d)):
        p = place[flip]
        rows = pl.ds(pl.multiple_of(p * quarter, quarter), quarter)
        for n, out in enumerate((wq, wk, wv)):
            out[rows] = ref[:, n * local : (n + 1) * local].astype(BF)


def unpack_qkv(place, parts, width, local):
    return pl.pallas_call(
        unpack_qkv_kernel,
        in_specs=[pl.BlockSpec(memory_space=pltpu.SMEM)]
        + [pl.BlockSpec(memory_space=pltpu.VMEM)] * 4,
        out_specs=[pl.BlockSpec(memory_space=pltpu.VMEM)] * 3,
        out_shape=[jax.ShapeDtypeStruct((width, local), BF)] * 3,
        compiler_params=params(),
        name="unpack_qkv",
    )(place, *parts)


def unpack_ff_kernel(place, a, b, c, d, wo, wi, wu):
    width, ff = wi.shape
    quarter, fourth, few = width // 4, ff // 4, wo.shape[0] // 4
    for flip, ref in ((0, a), (2, b), (1, c), (3, d)):
        p = place[flip]
        rows = pl.ds(pl.multiple_of(p * quarter, quarter), quarter)
        for n in range(ff // width):
            wi[rows, n * width : (n + 1) * width] = ref[
                n * quarter : (n + 1) * quarter
            ].astype(BF)
        base = quarter * (ff // width)
        wu[pl.ds(pl.multiple_of(p * fourth, fourth), fourth)] = ref[
            base : base + fourth
        ].astype(BF)
        wo[pl.ds(pl.multiple_of(p * few, few), few)] = ref[base + fourth :].astype(BF)


def unpack_ff(place, parts, width, local, ff):
    return pl.pallas_call(
        unpack_ff_kernel,
        in_specs=[pl.BlockSpec(memory_space=pltpu.SMEM)]
        + [pl.BlockSpec(memory_space=pltpu.VMEM)] * 4,
        out_specs=[pl.BlockSpec(memory_space=pltpu.VMEM)] * 3,
        out_shape=[
            jax.ShapeDtypeStruct((local, width), BF),
            jax.ShapeDtypeStruct((width, ff), BF),
            jax.ShapeDtypeStruct((ff, width), BF),
        ],
        compiler_params=params(),
        name="unpack_ff",
    )(place, *parts)


def flipped(size, bit):
    return [(i, i ^ bit) for i in range(size)]


def spread(chunk, dp):
    a = lax.ppermute(chunk, "mp", [(0, 1), (1, 0)])
    b = lax.ppermute(a, "dp", flipped(dp, 2))
    c = lax.ppermute(a, "dp", flipped(dp, 1))
    d = lax.ppermute(b, "dp", flipped(dp, 1))
    return a, b, c, d


def shards(
    dp, state, lengths, halt_mask, wq, wk, wv, wo, gain1, bias1, wi, wu, gain2, bias2,
    halt_weight, cotangent
):
    rows, width = state.shape
    local, ff = wq.shape[1], wi.shape[1]
    timing = jnp.asarray(timing_rows(width))
    me = lax.rem(lax.axis_index("dp"), 4).astype(jnp.int32)
    places = jnp.bitwise_xor(me, jnp.arange(4, dtype=jnp.int32))
    chunk_a, chunk_b = pack(places, wq, wk, wv, wo, wi, wu)
    parts_a = spread(chunk_a, dp)
    parts_b = spread(chunk_b, dp)
    e_a, mix_a, r_a = attention_forward(lengths, state, timing, wq, wk, wv)
    wq2, wk2, wv2 = unpack_qkv(places, parts_a, width, local)
    e_b, mix_b, r_b = attention_forward(lengths, state, timing, wq2, wk2, wv2)
    wo2, wi2, wu2 = unpack_ff(places, parts_b, width, local, ff)
    vectors = jnp.stack([gain1, bias1, gain2, bias2, halt_weight] + [gain1] * 3)
    new_state, gs, do_a, do_b, dl_a, dl_b, grads = middle(
        state, timing, cotangent, halt_mask[:, None], mix_a, mix_b, r_a, r_b, wo, wo2, wi,
        wi2, wu, wu2, vectors
    )
    gs, gq, gk, gv = attention_backward(e_a, do_a, dl_a, state, timing, wq, wk, wv, gs, True)
    (gs,) = attention_backward(e_b, do_b, dl_b, state, timing, wq2, wk2, wv2, gs, False)
    grads, gq, gk, gv = lax.psum((grads, gq, gk, gv), "dp")
    gi = jnp.concatenate([grads[ff + n * width : ff + (n + 1) * width] for n in range(ff // width)], axis=1)
    base = 2 * ff + local
    return (
        new_state,
        gs,
        gq,
        gk,
        gv,
        grads[2 * ff : base],
        grads[base],
        grads[base + 1],
        gi,
        grads[:ff],
        grads[base + 2],
        grads[base + 3],
        grads[base + 4],
    )


def solution(mesh):
    rows, columns, parts = P("dp", None), P(None, "mp"), P("mp", None)
    return jax.shard_map(
        functools.partial(shards, mesh.shape["dp"]),
        mesh=mesh,
        in_specs=(
            rows, P("dp"), P("dp"), columns, columns, columns, parts, P(), P(), columns,
            parts, P(), P(), P(), rows
        ),
        out_specs=(
            rows, rows, columns, columns, columns, parts, P(), P(), columns, parts, P(), P(),
            P()
        ),
        check_vma=False,
    )
```

time: 867 us -> 363 us (0.42)
  waiting for transfers between devices: 488 us -> 174 us
  matrix products: 152 us -> 0 us
  Pallas kernels: 0 us -> 150 us
  other arithmetic: 82 us -> 1.97 us
  blocking collectives: 61.1 us -> 0 us
  local copies, waits for them, and re-layouts: 62.9 us -> 14.3 us
    psum x5 -> x1, waiting for transfers between devices: 488 us -> 116 us  [shards(): grads, gq, gk, gv = lax.psum((grads, gq, gk, gv), 'dp')]
    dot_general x24 -> x0, matrix products: 152 us -> none  [the longest x1 24.4 us: shards(): jnp.einsum('sqhd,skhd->shqk', d_mixed4, value4, preferred_element_type=jn...]
    pallas_call x0 -> x8, Pallas kernels: none -> 150 us  [the longest x2 56.2 us: attention_backward(): pl.pallas_call(functools.partial(attention_backward_kernel, heads=heads,...]
    psum x1 -> x0, blocking collectives: 61.1 us -> none  [shards(): lax.psum((grad_query, grad_key, grad_value, grad_output, first_gain_gradi...]
    ppermute x0 -> x8, waiting for transfers between devices: none -> 58 us  [the longest x2 34.7 us: spread(): a = lax.ppermute(chunk, 'mp', [(0, 1), (1, 0)])]
    reduce_sum x8 -> x0, other arithmetic: 39.9 us -> none  [the longest x1 14.5 us: shards(): log_total = jax.nn.logsumexp(scores, axis=-1)]
    reshape x8 -> x0, local copies, waits for them, and re-layouts: 31.6 us -> none  [the longest x2 8.64 us: shards(): key4 = key.reshape(seqs, LEN, heads, HEAD)]
    convert_element_type x2 -> x0, other arithmetic: 28.5 us -> none  [the longest x1 27.8 us: shards(): (probs * (d_probs - jnp.sum(probs * d_probs, axis=-1, keepdims=True))).as...]
  transfers between devices with their start and end apart: 5 -> 9, of which waited for: 5 -> 4; matrix products, arithmetic and copies ran while one was open for 4% -> 1% of each run, Pallas kernels for 0% -> 18%
where the time goes in v1:
time: 363 us; the launch traced here: 362 us
  waiting for transfers between devices  174 us (48%)
  Pallas kernels  150 us (41%)
  local copies, waits for them, and re-layouts  14.3 us (4%)
  between operations  14.1 us (4%)
  starting transfers between devices  7.39 us (2%)
    psum x1, waiting for transfers between devices, shards(): grads, gq, gk, gv = lax.psum((grads, gq, gk, gv), 'dp')  116 us
    pallas_call x2, Pallas kernels, attention_backward(): pl.pallas_call(functools.partial(attention_backward_kernel, heads=heads,...  56.2 us
    pallas_call x1, Pallas kernels, middle(): pl.pallas_call(functools.partial(middle_kernel, heads=heads), grid=(rows...  47.3 us
    pallas_call x2, Pallas kernels, attention_forward(): pl.pallas_call(functools.partial(attention_forward_kernel, seqs=seqs, hea...  37.5 us
    ppermute x2, waiting for transfers between devices, spread(): a = lax.ppermute(chunk, 'mp', [(0, 1), (1, 0)])  34.7 us
    ppermute x2, waiting for transfers between devices, spread(): b = lax.ppermute(a, 'dp', flipped(dp, 2))  23.3 us
  transfers between devices with their start and end apart: 9, of which 4 were waited for; matrix products, arithmetic and copies ran while one was open for 1% of the time, Pallas kernels for 18%

profile of v1, /device:TPU:0, one launch (start us, length us, event | category | flops | bytes accessed | tf_op | source)
XLA Modules:
  0.0 362.4 jit_solution(13450293457162105327)
XLA Ops:
  7.2 0.0 all-reduce.3.cloned.1.call-start
  7.2 0.5 iota_xor_fusion.place
  7.7 3.0 pack.1
  10.8 2.9 collective-permute-start.4
  13.7 26.2 %collective-permute-done.4.a = f32[576,512]{1,0:T(8,128)S(1)} collective-permute-done((f32[576,512]{1,0:T(8,128)}, f32[576,512]{1,0:T(8,128)S(1)}, u32[]{:S(2)}, u32[]{:S(2)}) %collective-permute-start.4) | collective-permute-done | bytes 1179680 | tf_op jit(solution)/shard_map/ppermute | solution.py:595
  39.9 0.0 copy-start
  39.9 1.8 collective-permute-start.5
  41.7 0.0 copy-start.7
  41.7 0.0 copy-start.6
  41.7 0.0 copy-start.8
  41.7 1.5 collective-permute-start
  43.2 8.5 %collective-permute-done.a = f32[128,768]{1,0:T(8,128)} collective-permute-done((f32[128,768]{1,0:T(8,128)}, f32[128,768]{1,0:T(8,128)}, u32[]{:S(2)}, u32[]{:S(2)}) %collective-permute-start) | collective-permute-done | bytes 393248 | tf_op jit(solution)/shard_map/ppermute | solution.py:595
  51.7 0.6 collective-permute-start.1
  52.3 0.0 collective-permute-start.2
  52.3 23.3 %collective-permute-done.1.b = f32[128,768]{1,0:T(8,128)} collective-permute-done((f32[128,768]{1,0:T(8,128)}, f32[128,768]{1,0:T(8,128)}, u32[]{:S(2)}, u32[]{:S(2)}) %collective-permute-start.1) | collective-permute-done | bytes 393248 | tf_op jit(solution)/shard_map/ppermute | solution.py:596
  75.6 0.0 collective-permute-start.3
  75.6 0.5 collective-permute-start.6
  76.1 0.0 collective-permute-done.5.b
  76.1 0.0 copy-start.1
  76.1 0.1 collective-permute-start.7
  76.2 18.9 %attention_forward.2 = (bf16[8,1024,1024]{2,1,0:T(8,128)(2,1)}, bf16[256,2048]{1,0:T(8,128)(2,1)}, f32[8,1,1024]{2,1,0:T(1,128)}) custom-call(s32[2]{0:T(128)} %lengths.3, bf16[2048,512]{1,0:T(8,128)(2,1)} %state.9, f32[1024,512]{1,0:T(8,128)} %constant.13.clone.timing, bf16[512,256]{1,0:T(8,128)(2,1)} %wq.5, bf16[512,256]{1,0:T(8,128)(2,1)} %wk.5, ...), custom_call_target="tpu_custom_call" | custom-call | flops 8589934592 | bytes 16777216 | tf_op jit(solution)/shard_map/attention_forward/pallas_call | solution.py:148
  95.1 0.0 copy-done
  95.1 0.0 copy-done.1
  95.1 0.0 copy-done.7
  95.1 1.4 copy.31.run
  96.5 0.0 copy-done.6
  96.5 0.0 copy-done.8
  96.5 1.3 stack.26.vectors
  97.9 0.0 collective-permute-done.2.c
  97.9 0.0 collective-permute-done.3.d
  97.9 2.3 unpack_qkv.1
  100.2 18.6 %attention_forward.3 = (bf16[8,1024,1024]{2,1,0:T(8,128)(2,1)}, bf16[256,2048]{1,0:T(8,128)(2,1)}, f32[8,1,1024]{2,1,0:T(1,128)}) custom-call(s32[2]{0:T(128)} %lengths.3, bf16[2048,512]{1,0:T(8,128)(2,1)} %state.9, f32[1024,512]{1,0:T(8,128)} %constant.13.clone.timing, bf16[512,256]{1,0:T(8,128)(2,1)} %get-tuple-element.40.wq, ...), custom_call_target="tpu_custom_call" | custom-call | flops 8589934592 | bytes 16777216 | tf_op jit(solution)/shard_map/attention_forward/pallas_call | solution.py:148
  118.8 0.0 collective-permute-done.6.c
  118.8 0.0 copy-start.2
  118.8 0.0 collective-permute-done.7.d
  118.8 1.0 copy-done.2
  119.8 3.9 %unpack_ff.1 = (bf16[256,512]{1,0:T(8,128)(2,1)}, bf16[512,1024]{1,0:T(8,128)(2,1)}, bf16[1024,512]{1,0:T(8,128)(2,1)}) custom-call(s32[4]{0:T(128)} %iota_xor_fusion.place, f32[576,512]{1,0:T(8,128)} %copy-done, f32[576,512]{1,0:T(8,128)} %copy-done.1, f32[576,512]{1,0:T(8,128)} %copy-done.2, f32[576,512]{1,0:T(8,128)} %collective-permute-done.7.d), custom_call_target="tpu_custom_call" | custom-call | tf_op jit(solution)/shard_map/unpack_ff/pallas_call | solution.py:575
  123.7 47.3 %middle.1 = (f32[2048,512]{1,0:T(8,128)}, f32[2048,512]{1,0:T(8,128)}, f32[256,2048]{1,0:T(8,128)}, f32[256,2048]{1,0:T(8,128)}, f32[8,1,1024]{2,1,0:T(1,128)}, ...) custom-call(bf16[2048,512]{1,0:T(8,128)(2,1)} %state.9, f32[1024,512]{1,0:T(8,128)} %constant.13.clone.timing, ...), custom_call_target="tpu_custom_call" | custom-call | flops 24696061952 | bytes 20971520 | tf_op jit(solution)/shard_map/middle/pallas_call | solution.py:305
  171.0 29.6 %attention_backward_own.1 = (f32[2048,512]{1,0:T(8,128)}, f32[512,256]{1,0:T(8,128)}, f32[512,256]{1,0:T(8,128)}, f32[512,256]{1,0:T(8,128)}) custom-call(bf16[8,1024,1024]{2,1,0:T(8,128)(2,1)} %get-tuple-element.54.e_in, f32[256,2048]{1,0:T(8,128)} %get-tuple-element.55.do_in, ...), custom_call_target="tpu_custom_call", output_to_operand_aliasing={{0}: (8, {})} | custom-call | flops 17179869184 | bytes 16777216 | tf_op jit(solution)/shard_map/attention_backward_own/pallas_call | solution.py:471
  200.6 0.0 all-reduce.3.cloned.1.call-update
  200.6 26.6 %attention_backward_other.1 = f32[2048,512]{1,0:T(8,128)} custom-call(bf16[8,1024,1024]{2,1,0:T(8,128)(2,1)} %get-tuple-element.51.e_in, f32[256,2048]{1,0:T(8,128)} %get-tuple-element.52.do_in, f32[8,1,1024]{2,1,0:T(1,128)} %get-tuple-element.53.dl_in, bf16[2048,512]{1,0:T(8,128)(2,1)} %state.9, ...), custom_call_target="tpu_custom_call", output_to_operand_aliasing={{}: (8, {})} | custom-call | flops 17179869184 | bytes 16777216 | tf_op jit(solution)/shard_map/attention_backward_other/pallas_call | solution.py:471
  227.3 116.3 %all-reduce.3.cloned.1.call-done = (f32[512,256]{1,0:T(8,128)}, f32[512,256]{1,0:T(8,128)}, f32[512,256]{1,0:T(8,128)}, f32[2312,512]{1,0:T(8,128)}) async-done(((f32[512,256]{1,0:T(8,128)}, f32[512,256]{1,0:T(8,128)}, f32[512,256]{1,0:T(8,128)}, f32[2312,512]{1,0:T(8,128)}), (f32[512,256]{1,0:T(8,128)}, f32[512,256]{1,0:T(8,128)}, f32[512,256]{1,0:T(8,128)}, ...) | async-done | bytes 6307856 | tf_op jit(solution)/shard_map/psum | solution.py:625
  343.6 1.5 fusion
  345.1 1.9 slice.36
  346.9 3.1 slice.41
  350.0 1.7 fusion.1
  351.7 0.0 copy-start.5
  351.7 0.0 copy-start.4
  351.7 1.5 pad_maximum_fusion
  353.2 0.0 copy-start.3
  353.2 0.0 copy-done.5
  353.2 0.8 copy.38
  354.0 0.0 copy-done.4
  354.0 0.8 copy.39
  354.8 0.0 copy-done.3
  354.8 0.8 copy.40
Async XLA Ops:
  7.2 336.4 %all-reduce.3.cloned.1.call-start = ((), (), s32[]{:S(2)}) async-start(), calls=%async_computation | async-start | bytes 12615680 | tf_op jit(solution)/shard_map/psum | solution.py:625
  10.8 29.1 %collective-permute-start.4 = (f32[576,512]{1,0:T(8,128)}, f32[576,512]{1,0:T(8,128)S(1)}, u32[]{:S(2)}, u32[]{:S(2)}) collective-permute-start(f32[576,512]{1,0:T(8,128)} %get-tuple-element.46), channel_id=1, source_target_pairs={{0,1},{1,0},{2,3},{3,2},{4,5},{5,4},{6,7},{7,6},{8,9},{9,8},{10,11... | collective-permute-start | bytes 3538952 | tf_op jit(solution)/shard_map/ppermute | solution.py:595
  39.9 55.2 %copy-start = (f32[576,512]{1,0:T(8,128)}, f32[576,512]{1,0:T(8,128)S(1)}, u32[]{:S(2)}) copy-start(f32[576,512]{1,0:T(8,128)S(1)} %collective-permute-done.4.a) | copy-start | bytes 3538948
  39.9 36.2 %collective-permute-start.5 = (f32[576,512]{1,0:T(8,128)S(1)}, f32[576,512]{1,0:T(8,128)S(1)}, u32[]{:S(2)}, u32[]{:S(2)}) collective-permute-start(f32[576,512]{1,0:T(8,128)S(1)} %collective-permute-done.4.a), channel_id=1, source_target_pairs={{0,4},{2,6},{4,0},{6,2},{8,12},{10,14},{12,8},{14,10},{16,20},{18,... | collective-permute-start | bytes 3538952 | tf_op jit(solution)/shard_map/ppermute | solution.py:596
  41.7 53.5 %copy-start.7 = (s32[2048]{0:T(1024)S(1)}, s32[2048]{0:T(1024)}, u32[]{:S(2)}) copy-start(s32[2048]{0:T(1024)} %param.18) | copy-start | bytes 24580
  41.7 54.8 %copy-start.6 = (f32[512]{0:T(512)S(1)}, f32[512]{0:T(512)}, u32[]{:S(2)}) copy-start(f32[512]{0:T(512)} %param.23) | copy-start | bytes 6148
  41.7 54.8 %copy-start.8 = (f32[512]{0:T(512)S(1)}, f32[512]{0:T(512)}, u32[]{:S(2)}) copy-start(f32[512]{0:T(512)} %param.24) | copy-start | bytes 6148
  41.7 10.0 %collective-permute-start = (f32[128,768]{1,0:T(8,128)}, f32[128,768]{1,0:T(8,128)}, u32[]{:S(2)}, u32[]{:S(2)}) collective-permute-start(f32[128,768]{1,0:T(8,128)} %get-tuple-element.39), channel_id=1, source_target_pairs={{0,1},{1,0},{2,3},{3,2},{4,5},{5,4},{6,7},{7,6},{8,9},{9,8},{10,11... | collective-permute-start | bytes 1179656 | tf_op jit(solution)/shard_map/ppermute | solution.py:595
  51.7 23.9 %collective-permute-start.1 = (f32[128,768]{1,0:T(8,128)}, f32[128,768]{1,0:T(8,128)}, u32[]{:S(2)}, u32[]{:S(2)}) collective-permute-start(f32[128,768]{1,0:T(8,128)} %collective-permute-done.a), channel_id=1, source_target_pairs={{0,4},{2,6},{4,0},{6,2},{8,12},{10,14},{12,8},{14,10},{16,20},{18,... | collective-permute-start | bytes 1179656 | tf_op jit(solution)/shard_map/ppermute | solution.py:596
  52.3 45.6 %collective-permute-start.2 = (f32[128,768]{1,0:T(8,128)}, f32[128,768]{1,0:T(8,128)}, u32[]{:S(2)}, u32[]{:S(2)}) collective-permute-start(f32[128,768]{1,0:T(8,128)} %collective-permute-done.a), channel_id=1, source_target_pairs={{0,2},{2,0},{4,6},{6,4},{8,10},{10,8},{12,14},{14,12},{16,18},{18,... | collective-permute-start | bytes 1179656 | tf_op jit(solution)/shard_map/ppermute | solution.py:597
  75.6 22.3 %collective-permute-start.3 = (f32[128,768]{1,0:T(8,128)}, f32[128,768]{1,0:T(8,128)}, u32[]{:S(2)}, u32[]{:S(2)}) collective-permute-start(f32[128,768]{1,0:T(8,128)} %collective-permute-done.1.b), channel_id=1, source_target_pairs={{0,2},{2,0},{4,6},{6,4},{8,10},{10,8},{12,14},{14,12},{16,18},{18,... | collective-permute-start | bytes 1179656 | tf_op jit(solution)/shard_map/ppermute | solution.py:598
  75.6 43.2 %collective-permute-start.6 = (f32[576,512]{1,0:T(8,128)S(1)}, f32[576,512]{1,0:T(8,128)S(1)}, u32[]{:S(2)}, u32[]{:S(2)}) collective-permute-start(f32[576,512]{1,0:T(8,128)S(1)} %collective-permute-done.4.a), channel_id=1, source_target_pairs={{0,2},{2,0},{4,6},{6,4},{8,10},{10,8},{12,14},{14,12},{16,18},{18,... | collective-permute-start | bytes 3538952 | tf_op jit(solution)/shard_map/ppermute | solution.py:597
  76.1 19.0 %copy-start.1 = (f32[576,512]{1,0:T(8,128)}, f32[576,512]{1,0:T(8,128)S(1)}, u32[]{:S(2)}) copy-start(f32[576,512]{1,0:T(8,128)S(1)} %collective-permute-done.5.b) | copy-start | bytes 3538948
  76.1 42.7 %collective-permute-start.7 = (f32[576,512]{1,0:T(8,128)S(1)}, f32[576,512]{1,0:T(8,128)}, u32[]{:S(2)}, u32[]{:S(2)}) collective-permute-start(f32[576,512]{1,0:T(8,128)S(1)} %collective-permute-done.5.b), channel_id=1, source_target_pairs={{0,2},{2,0},{4,6},{6,4},{8,10},{10,8},{12,14},{14,12},{16,18},{18,... | collective-permute-start | bytes 3538952 | tf_op jit(solution)/shard_map/ppermute | solution.py:598
  118.8 1.0 copy-start.2
  351.7 1.5 copy-start.5
  351.7 2.3 copy-start.4
  353.2 1.6 copy-start.3
Sparse Core Ops, SparseCore 0:
  200.7 142.7 all-reduce.2
